TPU v7x, 128 devices: a whole 4x4x4 slice. The times are simulated.
128 devices in a mesh: dp: 32 (over z, x_lo, y), tensor: 4 (over x_hi, core).
Axes of the slice: x: 4 (x_hi: 2, x_lo: 2; x = x_hi * 2 + x_lo), y: 4, z: 4, core: 2. Of those that a mesh axis runs over, the one named last changes fastest.
Arguments:
- tokens: bfloat16 [16384, 1152], P(('dp', 'tensor')), may hold values from -6 to 6
- doc_lengths: int32 [16], replicated, may hold values from 1 to 2048, 16384 in all
- norm_gains: float32 [1152, 4], replicated, may hold values from -0.5 to 0.5
- head_gains: float32 [256, 2], replicated, may hold values from -0.5 to 0.5
- q_o: bfloat16 [1152, 2, 1024], P('dp', None, 'tensor'), may hold values from -0.1875 to 0.1875
- kv_weight: bfloat16 [1152, 512], P('dp'), may hold values from -0.1875 to 0.1875
- ffn_weight: bfloat16 [1152, 3, 6912], P('dp', None, 'tensor'), may hold values from -0.1875 to 0.1875
- out_grad: bfloat16 [16384, 1152], P(('dp', 'tensor')), may hold values from -6 to 6
Outputs:
- mixed: bfloat16 [16384, 1152], P(('dp', 'tensor'))
- tokens_grad: bfloat16 [16384, 1152], P(('dp', 'tensor'))
- norm_gains_grad: float32 [1152, 4], P('dp')
- head_gains_grad: float32 [256, 2], P('dp')
- q_o_grad: float32 [1152, 2, 1024], P('dp', None, 'tensor')
- kv_grad: float32 [1152, 512], P('dp')
- ffn_grad: float32 [1152, 3, 6912], P('dp', None, 'tensor')
Inputs may be any that keep to these rules, and one draw needn't show every extreme that they name: `doc_lengths`: the lengths sum to 16384; the longest is exactly 2048.
All inputs are finite; a program needn't handle non-finite values.
Results may differ from a plain program's by a relative error of at most 0.033.
Values may be sent and summed in bfloat16 or wider, within the bound.
No kernel may reach another device: no remote copies, remote signals or barrier semaphores. Data moves between devices by JAX's collectives and lax.ppermute only.
A program may use at most 128 MiB of HBM per device.

v0:
```python
import math

import jax
import jax.numpy as jnp
from jax import lax
from jax.sharding import PartitionSpec as P

WINDOW = 512


epsilon = 1e-06
rope_base = 10000.0
masked_score = -1e30


def in_one_piece(arrays, axis, dim, along):
    widths = [math.prod(a.shape[along:]) for a in arrays]
    both = jnp.concatenate(
        [a.reshape(*a.shape[:along], w) for a, w in zip(arrays, widths)], axis=along
    )
    whole = lax.all_gather(both, axis, axis=dim, tiled=True)
    tiles = jnp.split(whole, [sum(widths[:k]) for k in range(1, len(widths))], axis=along)
    return tuple((b.reshape(*whole.shape[:along], *a.shape[along:]) for a, b in zip(arrays, tiles)))


def in_order(tiles, dim):
    shape = list(tiles.shape[1:])
    shape[dim] *= tiles.shape[0]
    return jnp.moveaxis(tiles, 0, dim).reshape(shape)


def copy_for_each(array, axis):
    peers = lax.axis_size(axis)
    return lax.all_to_all(
        jnp.broadcast_to(array[None], (peers, *array.shape)), axis, 0, 0, tiled=True
    )


def gathered_copies(array, axis, dim):
    return in_order(copy_for_each(array, axis), dim)


def passed_along(array, axis, by):
    peers = lax.axis_size(axis)
    pairs = [(i, i + by) for i in range(peers) if 0 <= i + by < peers]
    return lax.ppermute(array, axis, pairs)


def cut_along(array, dim, peers):
    before, after = (array.shape[:dim], array.shape[dim + 1 :])
    return jnp.moveaxis(array.reshape(*before, peers, -1, *after), dim, 0)


def sum_at_owner(array, axis, dim):
    tiles = cut_along(array, dim, lax.axis_size(axis))
    arrived = lax.all_to_all(tiles, axis, split_axis=0, concat_axis=0, tiled=True)
    return arrived.astype(jnp.float32).sum(axis=0)


def rms_scale(values, gains):
    mean_square = jnp.mean(values * values, axis=-1, keepdims=True)
    return values * lax.rsqrt(mean_square + epsilon) * (1.0 + gains)


def norm_back(values, gains, upstream):
    inverse = lax.rsqrt(jnp.mean(values * values, axis=-1, keepdims=True) + epsilon)
    normed = values * inverse
    scaled = upstream * (1.0 + gains)
    grad_values = inverse * (scaled - normed * jnp.mean(scaled * normed, axis=-1, keepdims=True))
    return (grad_values, upstream * normed)


def rotate(values, cosine, sine_table):
    half_dim = values.shape[-1] // 2
    front = values[..., :half_dim]
    back_half = values[..., half_dim:]
    return jnp.concatenate(
        [front * cosine - back_half * sine_table, back_half * cosine + front * sine_table], axis=-1
    )


def rope_tables(position, head_dim):
    half_dim = head_dim // 2
    exponent = jnp.arange(half_dim).astype(jnp.float32) * (-2.0 / head_dim)
    frequency = jnp.power(jnp.float32(rope_base), exponent)
    angle = position.astype(jnp.float32)[:, None] * frequency[None, :]
    return (jnp.cos(angle), jnp.sin(angle))


def document_of(doc_lengths, index):
    ends = jnp.cumsum(doc_lengths)
    starts = ends - doc_lengths
    doc_number = jnp.sum((ends[None, :] <= index[:, None]).astype(jnp.int32), axis=1)
    owner = doc_number[:, None] == jnp.arange(doc_lengths.shape[0], dtype=jnp.int32)[None, :]
    position = index - jnp.sum(jnp.where(owner, starts[None, :], 0), axis=1)
    return (doc_number, position)


def geglu(gate_in, up_in):
    return jax.nn.gelu(gate_in, approximate=True) * up_in


def matmul(left, right):
    return jnp.dot(left, right, preferred_element_type=jnp.float32)


def matmul_nt(left, right):
    return lax.dot_general(
        left, right, (((1,), (1,)), ((), ())), preferred_element_type=jnp.float32
    )


def matmul_tn(left, right):
    return lax.dot_general(
        left, right, (((0,), (0,)), ((), ())), preferred_element_type=jnp.float32
    )


def body(tokens, doc_lengths, norm_gains, head_gains, q_o, kv_weight, ffn_weight, out_grad):
    rows_own = tokens.shape[0]
    group_rows = rows_own * lax.axis_size("tensor")
    head_dim = head_gains.shape[0]
    score_scale = head_dim ** (-0.5)
    own_start = lax.axis_index("tensor") * rows_own
    group_start = lax.axis_index("dp") * group_rows
    key_index = group_start - group_rows + jnp.arange(2 * group_rows, dtype=jnp.int32)
    key_doc, key_position = document_of(doc_lengths, key_index)
    key_doc = jnp.where(key_index < 0, -1, key_doc)
    query_index = key_index[group_rows:]
    query_doc = key_doc[group_rows:]
    cosine, sine_table = rope_tables(key_position[group_rows:], head_dim)
    distance = query_index[:, None] - key_index[None, :]
    allowed = (query_doc[:, None] == key_doc[None, :]) & (distance >= 0) & (distance < WINDOW)
    qo_full, kv_full = in_one_piece((q_o, kv_weight), "dp", 0, 1)
    ffn_full = lax.all_gather(ffn_weight, "dp", axis=0, tiled=True)
    w_query = qo_full[:, 0, :]
    w_output = qo_full[:, 1, :]
    w_gate = ffn_full[:, 0, :]
    w_up = ffn_full[:, 1, :]
    w_down = ffn_full[:, 2, :]
    inputs = tokens.astype(jnp.float32)
    normed_own = rms_scale(inputs, norm_gains[:, 0]).astype(jnp.bfloat16)
    normed = gathered_copies(normed_own, "tensor", 0)
    query_raw = matmul(normed, w_query)
    key_val = matmul(normed, kv_full)
    key_raw = key_val[:, :head_dim]
    query_rot = rotate(rms_scale(query_raw, head_gains[:, 0]), cosine, sine_table).astype(
        jnp.bfloat16
    )
    key_rot = rotate(rms_scale(key_raw, head_gains[:, 1]), cosine, sine_table).astype(jnp.bfloat16)
    packed = jnp.concatenate([key_rot, key_val[:, head_dim:].astype(jnp.bfloat16)], axis=1)
    earlier = passed_along(packed, "dp", 1)
    both_keys = jnp.concatenate([earlier, packed], axis=0)
    key_all = both_keys[:, :head_dim]
    value_all = both_keys[:, head_dim:]
    scores = jnp.where(allowed, matmul_nt(query_rot, key_all) * score_scale, masked_score)
    top_score = jnp.max(scores, axis=1, keepdims=True)
    weights = jnp.exp(scores - top_score)
    total = jnp.sum(weights, axis=1, keepdims=True)
    log_total = top_score + jnp.log(total)
    probs = (weights / total).astype(jnp.bfloat16)
    attended = matmul(probs, value_all).astype(jnp.bfloat16)
    attn_out = sum_at_owner(matmul_nt(attended, w_output).astype(jnp.bfloat16), "tensor", 0)
    resid = inputs + rms_scale(attn_out, norm_gains[:, 1])
    ffn_in_own = rms_scale(resid, norm_gains[:, 2]).astype(jnp.bfloat16)
    ffn_in = gathered_copies(ffn_in_own, "tensor", 0)
    gate_val = matmul(ffn_in, w_gate)
    up_val = matmul(ffn_in, w_up)
    hidden = geglu(gate_val, up_val).astype(jnp.bfloat16)
    ffn_out = sum_at_owner(matmul_nt(hidden, w_down).astype(jnp.bfloat16), "tensor", 0)
    mixed = resid + rms_scale(ffn_out, norm_gains[:, 3])
    upstream = out_grad.astype(jnp.float32)
    grad_ffn_out, gain_three = norm_back(ffn_out, norm_gains[:, 3], upstream)
    grad_ffn = gathered_copies(grad_ffn_out.astype(jnp.bfloat16), "tensor", 0)
    grad_hidden = matmul(grad_ffn, w_down)
    grad_w_down = matmul_tn(grad_ffn, hidden)
    unused_value, pull = jax.vjp(geglu, gate_val, up_val)
    grad_gate, grad_up = pull(grad_hidden)
    grad_gate = grad_gate.astype(jnp.bfloat16)
    grad_up = grad_up.astype(jnp.bfloat16)
    grad_ffn_in = sum_at_owner(
        (matmul_nt(grad_gate, w_gate) + matmul_nt(grad_up, w_up)).astype(jnp.bfloat16), "tensor", 0
    )
    grad_w_gate = matmul_tn(ffn_in, grad_gate)
    grad_w_up = matmul_tn(ffn_in, grad_up)
    grad_ffn_w = jnp.stack([grad_w_gate, grad_w_up, grad_w_down], axis=1)
    grad_from_ffn, gain_two = norm_back(resid, norm_gains[:, 2], grad_ffn_in)
    grad_resid = upstream + grad_from_ffn
    grad_attn_out, gain_one = norm_back(attn_out, norm_gains[:, 1], grad_resid)
    grad_attn = gathered_copies(grad_attn_out.astype(jnp.bfloat16), "tensor", 0)
    grad_attended = matmul(grad_attn, w_output).astype(jnp.bfloat16)
    grad_w_output = matmul_tn(grad_attn, attended)
    probs_full = jnp.exp(
        jnp.where(allowed, matmul_nt(query_rot, key_all) * score_scale, masked_score) - log_total
    )
    probs_low = probs_full.astype(jnp.bfloat16)
    grad_value_all = matmul_tn(probs_low, grad_attended)
    grad_probs = matmul_nt(grad_attended, value_all)
    inner = jnp.sum(probs_full * grad_probs, axis=1, keepdims=True)
    grad_scores = (probs_full * (grad_probs - inner)).astype(jnp.bfloat16)
    grad_query_rot = matmul(grad_scores, key_all) * score_scale
    grad_key_all = matmul_tn(grad_scores, query_rot) * score_scale
    grad_query_norm = rotate(grad_query_rot, cosine, -sine_table)
    grad_query_raw, gain_query = norm_back(query_raw, head_gains[:, 0], grad_query_norm)
    grad_query = grad_query_raw.astype(jnp.bfloat16)
    grad_w_query = matmul_tn(normed, grad_query)
    key_grads = jnp.concatenate([grad_key_all, grad_value_all], axis=1)
    later = passed_along(key_grads[:group_rows].astype(jnp.bfloat16), "dp", -1).astype(jnp.float32)
    own_keys = key_grads[group_rows:] + later
    summed = sum_at_owner(own_keys.astype(jnp.bfloat16), "tensor", 0)
    cosine_own = lax.dynamic_slice_in_dim(cosine, own_start, rows_own, 0)
    sine_own = lax.dynamic_slice_in_dim(sine_table, own_start, rows_own, 0)
    key_raw_own = lax.dynamic_slice_in_dim(key_raw, own_start, rows_own, 0)
    grad_key_norm = rotate(summed[:, :head_dim], cosine_own, -sine_own)
    grad_key_raw, gain_key_rows = norm_back(key_raw_own, head_gains[:, 1], grad_key_norm)
    gain_key = jnp.sum(gain_key_rows, axis=0)
    grad_kv = jnp.concatenate([grad_key_raw, summed[:, head_dim:]], axis=1).astype(jnp.bfloat16)
    grad_w_kv = matmul_tn(normed_own, grad_kv)
    kv_rows = matmul_nt(grad_kv, kv_full)
    grad_normed = (
        sum_at_owner(matmul_nt(grad_query, w_query).astype(jnp.bfloat16), "tensor", 0) + kv_rows
    )
    grad_from_norm, gain_zero = norm_back(inputs, norm_gains[:, 0], grad_normed)
    tokens_grad = (grad_resid + grad_from_norm).astype(jnp.bfloat16)
    norm_part = jnp.stack(
        [
            jnp.sum(gain_zero, axis=0),
            jnp.sum(gain_one, axis=0),
            jnp.sum(gain_two, axis=0),
            jnp.sum(gain_three, axis=0),
        ],
        axis=1,
    )
    head_part = jnp.stack([jnp.sum(gain_query, axis=0), gain_key], axis=1)
    grad_qo = jnp.stack([grad_w_query, grad_w_output], axis=1)
    qo_share, kv_share, ffn_share, norm_share, head_share = (
        lax.psum_scatter(
            grad_qo.astype(jnp.bfloat16), "dp", scatter_dimension=0, tiled=True
        ).astype(jnp.float32),
        lax.psum_scatter(
            grad_w_kv.astype(jnp.bfloat16), "dp", scatter_dimension=0, tiled=True
        ).astype(jnp.float32),
        lax.psum_scatter(
            grad_ffn_w.astype(jnp.bfloat16), "dp", scatter_dimension=0, tiled=True
        ).astype(jnp.float32),
        lax.psum_scatter(
            norm_part.astype(jnp.bfloat16), "dp", scatter_dimension=0, tiled=True
        ).astype(jnp.float32),
        lax.psum_scatter(
            head_part.astype(jnp.bfloat16), "dp", scatter_dimension=0, tiled=True
        ).astype(jnp.float32),
    )
    norm_total, head_total, kv_total = (
        lax.psum(norm_share.astype(jnp.bfloat16), "tensor").astype(jnp.float32),
        lax.psum(head_share.astype(jnp.bfloat16), "tensor").astype(jnp.float32),
        lax.psum(kv_share.astype(jnp.bfloat16), "tensor").astype(jnp.float32),
    )
    return (
        mixed.astype(jnp.bfloat16),
        tokens_grad,
        norm_total,
        head_total,
        qo_share,
        kv_total,
        ffn_share,
    )


def solution(mesh):
    return jax.shard_map(
        body,
        mesh=mesh,
        in_specs=(
            P(("dp", "tensor"), None),
            P(),
            P(),
            P(),
            P("dp", None, "tensor"),
            P("dp", None),
            P("dp", None, "tensor"),
            P(("dp", "tensor"), None),
        ),
        out_specs=(
            P(("dp", "tensor"), None),
            P(("dp", "tensor"), None),
            P("dp", None),
            P("dp", None),
            P("dp", None, "tensor"),
            P("dp", None),
            P("dp", None, "tensor"),
        ),
        check_vma=False,
    )
```

profile of v0, /device:TPU:1, one launch (start us, length us, event | category | flops | bytes accessed | tf_op | source)
XLA Modules:
  0.0 1097.8 jit_solution(7108770919961739084)
XLA Ops:
  23.8 124.2 %all-gather.6.cloned.1.call-done = bf16[32,36,1024]{2,1,0:T(8,128)(2,1)} async-done(((bf16[1,36,1024]{2,1,0:T(8,128)(2,1)}), bf16[32,36,1024]{2,1,0:T(8,128)(2,1)}) %all-gather.6.cloned.1.call-update) | async-done | bytes 2359312 | tf_op jit(solution)/shard_map/all_gather | solution.py:21
  167.0 6.0 collective-permute-done
  175.9 66.2 %all_to_all.45 = bf16[4,128,1152]{2,1,0:T(8,128)(2,1)S(1)} all-to-all(bf16[4,128,1152]{2,1,0:T(8,128)(2,1)S(1)} %bitcast.100), channel_id=1, replica_groups=mesh['dp'=32,'tensor'=4] {'tensor'}, dimensions={0} | all-to-all | bytes 2359296 | tf_op jit(solution)/shard_map/all_to_all | solution.py:56
  249.2 134.7 %all-gather.4.cloned.1.call-done = bf16[1152,3,1728]{2,1,0:T(4,128)(2,1)} async-done(((bf16[36,3,1728]{2,1,0:T(4,128)(2,1)}), bf16[1152,3,1728]{2,1,0:T(4,128)(2,1)}) %all-gather.4.cloned.1.call-update) | async-done | bytes 11943952 | tf_op jit(solution)/shard_map/all_gather | solution.py:135
  384.0 29.7 %fusion.101 = (bf16[1152,1,1728]{2,1,0:T(2,128)(2,1)}, bf16[1152,1,1728]{2,1,0:T(2,128)(2,1)}, bf16[1152,1,1728]{2,1,0:T(2,128)(2,1)}) fusion(bf16[1152,3,1728]{2,1,0:T(4,128)(2,1)} %all-gather.4.cloned.1.call-done), kind=kLoop, calls=%fused_computation.208 | loop fusion | bytes 23887872 | tf_op jit(solution)/shard_map/slice | solution.py:140
  413.6 17.8 %copy.59 = bf16[1152,1,1728]{0,2,1:T(8,128)(2,1)} copy(bf16[1152,1,1728]{2,1,0:T(2,128)(2,1)} %get-tuple-element.70) | data formatting | bytes 7962624
  431.4 17.8 %copy.60 = bf16[1152,1,1728]{0,2,1:T(8,128)(2,1)} copy(bf16[1152,1,1728]{2,1,0:T(2,128)(2,1)} %get-tuple-element.69) | data formatting | bytes 7962624
  449.3 17.8 %copy.61 = bf16[1152,1,1728]{0,2,1:T(8,128)(2,1)} copy(bf16[1152,1,1728]{2,1,0:T(2,128)(2,1)} %get-tuple-element.68) | data formatting | bytes 7962624
  472.2 7.4 multiply_convert_fusion.1
  482.2 27.6 %all_to_all.46 = bf16[4,128,1152]{2,1,0:T(8,128)(2,1)S(1)} all-to-all(bf16[4,128,1152]{2,1,0:T(8,128)(2,1)S(1)} %bitcast.101), channel_id=1, replica_groups=mesh['dp'=32,'tensor'=4] {'tensor'}, dimensions={0} | all-to-all | bytes 2359296 | tf_op jit(solution)/shard_map/all_to_all | solution.py:56
  518.7 16.5 %all-to-all-done.4 = bf16[4,128,1152]{2,1,0:T(8,128)(2,1)} async-done(((bf16[4,128,1152]{2,1,0:T(8,128)(2,1)}), bf16[4,128,1152]{2,1,0:T(8,128)(2,1)}, u32[]{:S(2)}, u32[]{:S(2)}) %all-to-all-start.4) | async-done | bytes 1179680 | tf_op jit(solution)/shard_map/all_to_all | solution.py:34
  535.3 6.3 fusion.3
  541.6 6.4 fusion.22
  560.2 6.3 fusion.1
  587.3 10.2 pad_maximum_fusion
  597.5 27.0 %copy.51 = bf16[1152,3,1728]{2,1,0:T(4,128)(2,1)} copy(bf16[1152,3,1728]{0,2,1:T(8,128)(2,1)} %pad_maximum_fusion) | data formatting | bytes 23887872 | tf_op jit(solution)/shard_map/stack | solution.py:186
  634.8 8.3 copy.50
  658.1 22.2 %collective-permute-done.1 = bf16[512,512]{0,1:T(8,128)(2,1)S(1)} collective-permute-done((bf16[512,512]{0,1:T(8,128)(2,1)S(1)}, bf16[512,512]{0,1:T(8,128)(2,1)S(1)}, u32[]{:S(2)}, u32[]{:S(2)}) %collective-permute-start.1) | collective-permute-done | bytes 524320 | tf_op jit(solution)/shard_map/ppermute | solution.py:46
  691.8 11.1 %all-to-all-done.8 = bf16[4,128,512]{1,2,0:T(8,128)(2,1)S(1)} async-done(((bf16[4,128,512]{1,2,0:T(8,128)(2,1)}), bf16[4,128,512]{1,2,0:T(8,128)(2,1)S(1)}, u32[]{:S(2)}, u32[]{:S(2)}) %all-to-all-start.8) | async-done | bytes 524320 | tf_op jit(solution)/shard_map/all_to_all | solution.py:56
  708.2 102.9 %fusion = bf16[40,512]{1,0:T(8,128)(2,1)S(1)} fusion(bf16[1152,512]{1,0:T(8,128)(2,1)} %convolution_convert_fusion.5), kind=kCustom, calls=%all-reduce-scatter | all-reduce-scatter fusion | flops 655361 | bytes 1221120
  816.7 7.8 collective-permute-start.5
  828.3 136.5 %all-reduce.6 = (bf16[1152,4]{0,1:T(4,128)(2,1)S(1)}, bf16[256,2]{0,1:T(2,128)(2,1)S(1)}) all-reduce(bf16[1152,4]{0,1:T(4,128)(2,1)S(1)} %pad_maximum_fusion.12, bf16[256,2]{0,1:T(2,128)(2,1)S(1)} %pad_maximum_fusion.13), channel_id=2, replica_groups=mesh['dp'=32,'tensor'=4] {'dp'}, use_global_device_ids=true, to_apply=%region_28.29.clone | all-reduce | flops 5120 | bytes 20480
  968.9 41.3 %all-reduce.8 = (bf16[36,4]{0,1:T(4,128)(2,1)S(1)}, bf16[8,2]{0,1:T(2,128)(2,1)S(1)}, bf16[36,512]{1,0:T(8,128)(2,1)S(1)}) all-reduce(bf16[36,4]{0,1:T(4,128)(2,1)S(1)} %constant_dynamic-slice_fusion.2, bf16[8,2]{0,1:T(2,128)(2,1)S(1)} %constant_dynamic-slice_fusion.1, ...), channel_id=1, replica_groups=mesh['dp'=32,'tensor'=4] {'tensor'}, use_global_device_ids=true, to_apply=%region_29.30 | all-reduce | flops 18592 | bytes 74368 | tf_op jit(solution)/shard_map/psum | solution.py:254
  1012.0 75.5 %all-reduce.11.cloned.1.call-done = (bf16[1152,2,256]{2,1,0:T(2,128)(2,1)}, bf16[1152,3,1728]{2,1,0:T(4,128)(2,1)}) async-done(((bf16[1152,2,256]{2,1,0:T(2,128)(2,1)}, bf16[1152,3,1728]{2,1,0:T(4,128)(2,1)}), (bf16[1152,2,256]{2,1,0:T(2,128)(2,1)}, bf16[1152,3,1728]{2,1,0:T(4,128)(2,1)})) %all-reduce.11.cloned.1.call-update) | async-done | bytes 13123600
  (266 shorter events, 153.5 us)
Async XLA Ops:
  7.2 140.9 %all-gather.6.cloned.1.call-start = ((), (), s32[]{:S(2)}) async-start(), calls=%async_computation.10 | async-start | bytes 2703360 | tf_op jit(solution)/shard_map/all_gather | solution.py:21
  9.5 374.4 %all-gather.4.cloned.1.call-start = ((), (), s32[]{:S(2)}) async-start(), calls=%async_computation.9 | async-start | bytes 17031168 | tf_op jit(solution)/shard_map/all_gather | solution.py:135
  15.8 139.1 %all-to-all-start = ((bf16[4,128,1152]{2,1,0:T(8,128)(2,1)}), bf16[4,128,1152]{2,1,0:T(8,128)(2,1)}, u32[]{:S(2)}, u32[]{:S(2)}) async-start(bf16[4,128,1152]{2,1,0:T(8,128)(2,1)} %broadcast_in_dim.29), calls=%async_computation | async-start | bytes 2359296 | tf_op jit(solution)/shard_map/all_to_all | solution.py:34
  161.6 470.3 %copy-start.36 = (f32[512]{0:T(512)}, f32[512]{0:T(512)S(1)}, u32[]{:S(2)}) copy-start(f32[512]{0:T(512)S(1)} %add_rsqrt_fusion.1) | copy-start | bytes 6148
  164.1 8.9 collective-permute-start
  175.9 66.5 %copy-start.10 = (bf16[128,1152]{1,0:T(8,128)(2,1)S(1)}, bf16[128,1152]{1,0:T(8,128)(2,1)}, u32[]{:S(2)}) copy-start(bf16[128,1152]{1,0:T(8,128)(2,1)} %param.8) | copy-start | bytes 884740
  243.9 223.2 %all-to-all-start.2 = ((bf16[4,128,1152]{2,1,0:T(8,128)(2,1)}), bf16[4,128,1152]{2,1,0:T(8,128)(2,1)}, u32[]{:S(2)}, u32[]{:S(2)}) async-start(bf16[4,128,1152]{2,1,0:T(8,128)(2,1)} %broadcast_in_dim.34), calls=%async_computation.2 | async-start | bytes 2359296 | tf_op jit(solution)/shard_map/all_to_all | solution.py:34
  512.9 22.3 %all-to-all-start.4 = ((bf16[4,128,1152]{2,1,0:T(8,128)(2,1)}), bf16[4,128,1152]{2,1,0:T(8,128)(2,1)}, u32[]{:S(2)}, u32[]{:S(2)}) async-start(bf16[4,128,1152]{2,1,0:T(8,128)(2,1)} %broadcast_in_dim.35), calls=%async_computation.4 | async-start | bytes 2359296 | tf_op jit(solution)/shard_map/all_to_all | solution.py:34
  518.7 110.3 %copy-start.34 = (f32[512]{0:T(512)}, f32[512]{0:T(512)S(1)}, u32[]{:S(2)}) copy-start(f32[512]{0:T(512)S(1)} %log_add_fusion) | copy-start | bytes 6148
  555.1 21.7 %all-to-all-start.5 = ((bf16[4,128,1152]{2,1,0:T(8,128)(2,1)}), bf16[4,128,1152]{2,1,0:T(8,128)(2,1)}, u32[]{:S(2)}, u32[]{:S(2)}) async-start(bf16[4,128,1152]{2,1,0:T(8,128)(2,1)} %bitcast.99), calls=%async_computation.5 | async-start | bytes 2359296 | tf_op jit(solution)/shard_map/all_to_all | solution.py:56
  582.1 42.5 %all-to-all-start.6 = ((bf16[4,128,1152]{2,1,0:T(8,128)(2,1)}), bf16[4,128,1152]{2,1,0:T(8,128)(2,1)}, u32[]{:S(2)}, u32[]{:S(2)}) async-start(bf16[4,128,1152]{2,1,0:T(8,128)(2,1)} %broadcast_in_dim.36), calls=%async_computation.6 | async-start | bytes 2359296 | tf_op jit(solution)/shard_map/all_to_all | solution.py:34
  587.2 500.3 %all-reduce.11.cloned.1.call-start = ((), (), s32[]{:S(2)}) async-start(), calls=%async_computation.11 | async-start | bytes 35389440
  646.0 36.3 %all-to-all-start.7 = ((bf16[4,128,1152]{2,1,0:T(8,128)(2,1)}), bf16[4,128,1152]{2,1,0:T(8,128)(2,1)}, u32[]{:S(2)}, u32[]{:S(2)}) async-start(bf16[4,128,1152]{2,1,0:T(8,128)(2,1)} %bitcast.16), calls=%async_computation.7 | async-start | bytes 2359296 | tf_op jit(solution)/shard_map/all_to_all | solution.py:56
  653.3 27.0 %collective-permute-start.1 = (bf16[512,512]{0,1:T(8,128)(2,1)S(1)}, bf16[512,512]{0,1:T(8,128)(2,1)S(1)}, u32[]{:S(2)}, u32[]{:S(2)}) collective-permute-start(bf16[512,512]{0,1:T(8,128)(2,1)S(1)} %fusion.43), channel_id=1, source_target_pairs={{4,0},{8,4},{12,8},{16,12},{20,16},{24,20},{28,24},{32,28},{36,32}... | collective-permute-start | bytes 1572872 | tf_op jit(solution)/shard_map/ppermute | solution.py:46
  658.1 30.2 %copy-start.47 = (bf16[1152]{0:T(1024)(128)(2,1)S(1)}, bf16[1152]{0:T(1024)(128)(2,1)}, u32[]{:S(2)}) copy-start(bf16[1152]{0:T(1024)(128)(2,1)} %get-tuple-element.44) | copy-start | bytes 6916
  682.2 20.7 %all-to-all-start.8 = ((bf16[4,128,512]{1,2,0:T(8,128)(2,1)}), bf16[4,128,512]{1,2,0:T(8,128)(2,1)S(1)}, u32[]{:S(2)}, u32[]{:S(2)}) async-start(bf16[4,128,512]{1,2,0:T(8,128)(2,1)} %copy_bitcast_fusion.2), calls=%async_computation.8 | async-start | bytes 1048576 | tf_op jit(solution)/shard_map/all_to_all | solution.py:56
  702.9 122.3 %copy-start.4 = (bf16[1152,1024]{1,0:T(8,128)(2,1)S(1)}, bf16[1152,1024]{1,0:T(8,128)(2,1)}, u32[]{:S(2)}) copy-start(bf16[1152,1024]{1,0:T(8,128)(2,1)} %copy-done.3) | copy-start | bytes 7077892
  703.0 122.3 %copy-start.11 = (bf16[128,1152]{1,0:T(8,128)(2,1)S(1)}, bf16[128,1152]{1,0:T(8,128)(2,1)}, u32[]{:S(2)}) copy-start(bf16[128,1152]{1,0:T(8,128)(2,1)} %param.8) | copy-start | bytes 884740
  703.0 122.3 %copy-start.30 = (f32[1152]{0:T(1024)S(1)}, f32[1152]{0:T(1024)}, u32[]{:S(2)}) copy-start(f32[1152]{0:T(1024)} %copy-done.29) | copy-start | bytes 13828
  708.2 257.4 %copy-start.6 = (f32[128,1152]{1,0:T(8,128)S(1)}, f32[128,1152]{1,0:T(8,128)}, u32[]{:S(2)}) copy-start(f32[128,1152]{1,0:T(8,128)} %copy-done.5) | copy-start | bytes 1769476
  811.1 156.5 %collective-permute-start.2 = (bf16[40,512]{1,0:T(8,128)(2,1)S(1)}, bf16[40,512]{1,0:T(8,128)(2,1)S(1)}, u32[]{:S(2)}, u32[]{:S(2)}) collective-permute-start(bf16[40,512]{1,0:T(8,128)(2,1)S(1)} %fusion), channel_id=1, source_target_pairs={{0,4},{4,8},{8,12},{12,16},{16,20},{20,24},{24,28},{28,32},{32,36}... | collective-permute-start | bytes 122888
  812.5 155.1 %collective-permute-start.3 = (bf16[40,512]{1,0:T(8,128)(2,1)S(1)}, bf16[40,512]{1,0:T(8,128)(2,1)S(1)}, u32[]{:S(2)}, u32[]{:S(2)}) collective-permute-start(bf16[40,512]{1,0:T(8,128)(2,1)S(1)} %fusion), channel_id=1, source_target_pairs={{0,8},{4,12},{8,16},{12,20},{16,24},{20,28},{24,32},{28,36},{32,40... | collective-permute-start | bytes 122888
  813.8 153.8 %collective-permute-start.4 = (bf16[40,512]{1,0:T(8,128)(2,1)S(1)}, bf16[40,512]{1,0:T(8,128)(2,1)S(1)}, u32[]{:S(2)}, u32[]{:S(2)}) collective-permute-start(bf16[40,512]{1,0:T(8,128)(2,1)S(1)} %fusion), channel_id=1, source_target_pairs={{0,12},{4,16},{8,20},{12,24},{16,28},{20,32},{24,36},{28,40},{32,4... | collective-permute-start | bytes 122888
  816.7 150.9 %collective-permute-start.5 = (bf16[4,512]{1,0:T(4,128)(2,1)}, bf16[4,512]{1,0:T(4,128)(2,1)}, u32[]{:S(2)}, u32[]{:S(2)}) collective-permute-start(bf16[4,512]{1,0:T(4,128)(2,1)} %slice.148), channel_id=1, source_target_pairs={{0,16},{4,20},{8,24},{12,28},{16,32},{20,36},{24,40},{28,44},{32,4... | collective-permute-start | bytes 12296
  (53 other events, 382.6 us)
Sparse Core Ops, SparseCore 0:
  10.2 137.7 all-gather.5
  150.3 233.6 all-gather.3
  643.2 444.2 all-reduce.10
where the time goes:
time: 1110 us; the launch traced here: 1100 us
  waiting for transfers between devices  395 us (36%)
  blocking collectives  374 us (34%)
  local copies, waits for them, and re-layouts  144 us (13%)
  matrix products  68.9 us (6%)
  starting transfers between devices  54.7 us (5%)
  other arithmetic  44.2 us (4%)
  between operations  16.9 us (2%)
    unnamed x2, blocking collectives  239 us
    all_gather x1, waiting for transfers between devices, body(): ffn_full = lax.all_gather(ffn_weight, 'dp', axis=0, tiled=True)  135 us
    all_gather x1, waiting for transfers between devices, in_one_piece(): whole = lax.all_gather(both, axis, axis=dim, tiled=True)  124 us
    all_to_all x2, blocking collectives, sum_at_owner(): lax.all_to_all(tiles, axis, split_axis=0, concat_axis=0, tiled=True)  93.7 us
    unnamed x8, waiting for transfers between devices  75.5 us
    unnamed x136, local copies, waits for them, and re-layouts  65.9 us
    psum x1, blocking collectives, body(): lax.psum(norm_share.astype(jnp.bfloat16), 'tensor').astype(jnp.float32)  41.3 us
    slice x1, local copies, waits for them, and re-layouts, body(): w_down = ffn_full[:, 2, :]  29.7 us
  transfers between devices with their start and end apart: 16, of which 8 were waited for; matrix products, arithmetic and copies ran while one was open for 26% of the time, Pallas kernels for 0%

commit v1 on v0

v1 whole, which is shorter than its diff:
```python
import jax
import jax.numpy as jnp
import numpy as np
from jax import lax
from jax.sharding import Mesh
from jax.sharding import PartitionSpec as P

WINDOW = 512
NZ, NXL, NY, NXH, NC = 4, 2, 4, 2, 2
ALL = ("z", "xl", "y", "xh", "c")
ZY = ("z", "y")
BLOCKS = NZ * NXL * NY * NXH * NC

epsilon = 1e-06
rope_base = 10000.0
masked_score = -1e30
bf16 = jnp.bfloat16
f32 = jnp.float32


def rms_scale(values, gains):
    mean_square = jnp.mean(values * values, axis=-1, keepdims=True)
    return values * lax.rsqrt(mean_square + epsilon) * (1.0 + gains)


def norm_back(values, gains, upstream):
    inverse = lax.rsqrt(jnp.mean(values * values, axis=-1, keepdims=True) + epsilon)
    normed = values * inverse
    scaled = upstream * (1.0 + gains)
    grad_values = inverse * (scaled - normed * jnp.mean(scaled * normed, axis=-1, keepdims=True))
    return (grad_values, upstream * normed)


def rotate(values, cosine, sine_table):
    half_dim = values.shape[-1] // 2
    front = values[..., :half_dim]
    back_half = values[..., half_dim:]
    return jnp.concatenate(
        [front * cosine - back_half * sine_table, back_half * cosine + front * sine_table], axis=-1
    )


def rope_tables(position, head_dim):
    half_dim = head_dim // 2
    exponent = jnp.arange(half_dim).astype(f32) * (-2.0 / head_dim)
    frequency = jnp.power(f32(rope_base), exponent)
    angle = position.astype(f32)[:, None] * frequency[None, :]
    return (jnp.cos(angle), jnp.sin(angle))


def document_of(doc_lengths, index):
    ends = jnp.cumsum(doc_lengths)
    starts = ends - doc_lengths
    doc_number = jnp.sum((ends[None, :] <= index[:, None]).astype(jnp.int32), axis=1)
    owner = doc_number[:, None] == jnp.arange(doc_lengths.shape[0], dtype=jnp.int32)[None, :]
    position = index - jnp.sum(jnp.where(owner, starts[None, :], 0), axis=1)
    return (doc_number, position)


def geglu(gate_in, up_in):
    return jax.nn.gelu(gate_in, approximate=True) * up_in


def matmul(left, right):
    return jnp.dot(left, right, preferred_element_type=f32)


def matmul_nt(left, right):
    return lax.dot_general(left, right, (((1,), (1,)), ((), ())), preferred_element_type=f32)


def matmul_tn(left, right):
    return lax.dot_general(left, right, (((0,), (0,)), ((), ())), preferred_element_type=f32)


def swap(array, axis):
    return lax.ppermute(array, axis, [(0, 1), (1, 0)])


def swap_both(array):
    return lax.ppermute(array, ("xl", "xh"), [(0, 3), (1, 2), (2, 1), (3, 0)])


def shifted(array, by):
    return lax.ppermute(
        array, ALL, [(i, i + by) for i in range(BLOCKS) if 0 <= i + by < BLOCKS]
    )


def group_rows(own):
    pair = jnp.concatenate([own, swap(own, "xh")], axis=0)
    return jnp.concatenate([pair, swap(pair, "c")], axis=0)


def group_sum(part):
    half = part.shape[0] // 2
    mine = part[:half].astype(f32) + swap(part[half:], "c").astype(f32)
    mine = mine.astype(bf16)
    own = half // 2
    return mine[:own].astype(f32) + swap(mine[own:], "xh").astype(f32)


def body(tokens, doc_lengths, norm_gains, head_gains, q_o, kv_weight, ffn_weight, out_grad):
    rows = tokens.shape[0]
    dim = tokens.shape[1]
    head_dim = head_gains.shape[0]
    score_scale = head_dim ** (-0.5)
    xl = lax.axis_index("xl")
    c = lax.axis_index("c")
    dp_rows = q_o.shape[0]
    ff = ffn_weight.shape[2]
    ff_pad = -ff % 256
    wide = ff + ff_pad

    ffn_own = jnp.pad(ffn_weight, ((0, 0), (0, 0), (0, ff_pad))).reshape(dp_rows, 3 * wide)
    ffn_pair = jnp.concatenate([ffn_own, swap(ffn_own, "xl")], axis=0)
    kv_half = lax.dynamic_slice_in_dim(kv_weight, c * head_dim, head_dim, 1)
    q_own, o_own = q_o[:, 0, :], q_o[:, 1, :]
    small = jnp.concatenate([q_own, kv_half, o_own], axis=1)
    from_xl, from_xh, from_both = swap(small, "xl"), swap(small, "xh"), swap_both(small)

    def beside(first, second):
        return jnp.concatenate(
            [
                first[:, :head_dim],
                second[:, :head_dim],
                first[:, head_dim : 2 * head_dim],
                first[:, 2 * head_dim :],
                second[:, 2 * head_dim :],
            ],
            axis=1,
        )

    attn_pair = jnp.concatenate([beside(small, from_xh), beside(from_xl, from_both)], axis=0)
    attn_a = lax.all_to_all(
        jnp.broadcast_to(attn_pair[None], (NZ * NY, *attn_pair.shape)), ZY, 0, 0, tiled=True
    ).reshape(dim, -1)
    attn_b = swap(attn_a, "c")
    ffn_full = lax.all_gather(ffn_pair, ZY, axis=0, tiled=True)

    new = jnp.arange(dim, dtype=jnp.int32)
    z_of, y_of = new // (dp_rows * NXL * NY), (new // (dp_rows * NXL)) % NY
    xl_of = jnp.bitwise_xor((new // dp_rows) % NXL, xl)
    old = ((z_of * NXL + xl_of) * NY + y_of) * dp_rows + new % dp_rows
    order = (jnp.arange(dim, dtype=jnp.int32)[:, None] == old[None, :]).astype(bf16)

    def reordered(array):
        tail = array.shape[1:]
        cut = array.reshape(NZ, NXL, NY, dp_rows, *tail)
        first = jnp.where(xl == 0, cut[:, 0], cut[:, 1])
        second = jnp.where(xl == 0, cut[:, 1], cut[:, 0])
        return jnp.stack([first, second], axis=2).reshape(dim, *tail)

    gains = reordered(norm_gains)
    inputs = matmul(tokens, order)
    upstream = matmul(out_grad, order)

    block = ((lax.axis_index("z") * NXL + xl) * NY + lax.axis_index("y")) * NXH * NC
    block = block + lax.axis_index("xh") * NC + c
    back = WINDOW // rows
    key_index = (block - back) * rows + jnp.arange((back + 1) * rows, dtype=jnp.int32)
    key_doc, key_position = document_of(doc_lengths, key_index)
    key_doc = jnp.where(key_index < 0, -1, key_doc)
    query_index = key_index[back * rows :]
    query_doc = key_doc[back * rows :]
    cosine, sine_table = rope_tables(key_position[back * rows :], head_dim)
    distance = query_index[:, None] - key_index[None, :]
    allowed = (query_doc[:, None] == key_doc[None, :]) & (distance >= 0) & (distance < WINDOW)

    normed = rms_scale(inputs, gains[:, 0]).astype(bf16)
    qkv_a = matmul(normed, attn_a[:, : 3 * head_dim])
    qkv_b = matmul(normed, attn_b[:, : 3 * head_dim])
    query_raw = jnp.stack(
        [
            qkv_a[:, :head_dim],
            qkv_a[:, head_dim : 2 * head_dim],
            qkv_b[:, :head_dim],
            qkv_b[:, head_dim : 2 * head_dim],
        ],
        axis=0,
    )
    kv_a, kv_b = qkv_a[:, 2 * head_dim :], qkv_b[:, 2 * head_dim :]
    key_raw = jnp.where(c == 0, kv_a, kv_b)
    value_low = jnp.where(c == 0, kv_b, kv_a).astype(bf16)
    key_rot = rotate(rms_scale(key_raw, head_gains[:, 1]), cosine, sine_table).astype(bf16)
    packed = jnp.concatenate([key_rot, value_low], axis=1)
    both = jnp.concatenate([shifted(packed, by) for by in range(back, 0, -1)] + [packed], axis=0)
    key_all, value_all = both[:, :head_dim], both[:, head_dim:]
    query_rot = rotate(rms_scale(query_raw, head_gains[:, 0]), cosine, sine_table).astype(bf16)
    heads = query_raw.shape[0]
    query_flat = query_rot.reshape(heads * rows, head_dim)
    scores = matmul_nt(query_flat, key_all).reshape(heads, rows, -1) * score_scale
    scores = jnp.where(allowed[None], scores, masked_score)
    top_score = jnp.max(scores, axis=2, keepdims=True)
    weights = jnp.exp(scores - top_score)
    total = jnp.sum(weights, axis=2, keepdims=True)
    probs_full = (weights / total).reshape(heads * rows, -1)
    probs = probs_full.astype(bf16)
    attended = matmul(probs, value_all).astype(bf16).reshape(heads, rows, head_dim)
    attended_a = jnp.concatenate([attended[0], attended[1]], axis=1)
    attended_b = jnp.concatenate([attended[2], attended[3]], axis=1)
    out_a, out_b = attn_a[:, 3 * head_dim :], attn_b[:, 3 * head_dim :]
    attn_out = matmul_nt(attended_a, out_a) + matmul_nt(attended_b, out_b)
    resid = inputs + rms_scale(attn_out, gains[:, 1])

    ffn_in = group_rows(rms_scale(resid, gains[:, 2]).astype(bf16))
    w_gate, w_up, w_down = ffn_full[:, :wide], ffn_full[:, wide : 2 * wide], ffn_full[:, 2 * wide :]
    gate_up = matmul(ffn_in, ffn_full[:, : 2 * wide])
    gate_val, up_val = gate_up[:, :wide], gate_up[:, wide:]
    hidden = geglu(gate_val, up_val).astype(bf16)
    ffn_out = group_sum(matmul_nt(hidden, w_down).astype(bf16))
    mixed = (resid + rms_scale(ffn_out, gains[:, 3])).astype(bf16)
    grad_ffn_out, gain_three = norm_back(ffn_out, gains[:, 3], upstream)
    grad_ffn = group_rows(grad_ffn_out.astype(bf16))
    grad_hidden = matmul(grad_ffn, w_down)
    unused_value, pull = jax.vjp(geglu, gate_val, up_val)
    grad_gate, grad_up = pull(grad_hidden)
    grad_gate_up = jnp.concatenate([grad_gate.astype(bf16), grad_up.astype(bf16)], axis=1)
    grad_ffn_in = group_sum(matmul_nt(grad_gate_up, ffn_full[:, : 2 * wide]).astype(bf16))
    grad_w = jnp.concatenate(
        [matmul_tn(ffn_in, grad_gate_up).astype(bf16), matmul_tn(grad_ffn, hidden).astype(bf16)],
        axis=1,
    )
    ffn_rows = lax.psum_scatter(grad_w, ZY, scatter_dimension=0, tiled=True)

    grad_from_ffn, gain_two = norm_back(resid, gains[:, 2], grad_ffn_in)
    grad_resid = upstream + grad_from_ffn
    grad_attn_out, gain_one = norm_back(attn_out, gains[:, 1], grad_resid)
    grad_attn = grad_attn_out.astype(bf16)

    att_grad_a = matmul(grad_attn, out_a).astype(bf16)
    att_grad_b = matmul(grad_attn, out_b).astype(bf16)
    grad_attended = jnp.concatenate(
        [
            att_grad_a[:, :head_dim],
            att_grad_a[:, head_dim:],
            att_grad_b[:, :head_dim],
            att_grad_b[:, head_dim:],
        ],
        axis=0,
    )
    grad_value_all = matmul_tn(probs, grad_attended)
    grad_probs = matmul_nt(grad_attended, value_all)
    inner = jnp.sum(probs_full * grad_probs, axis=1, keepdims=True)
    grad_scores = (probs_full * (grad_probs - inner)).astype(bf16)
    grad_query_rot = (matmul(grad_scores, key_all) * score_scale).reshape(heads, rows, head_dim)
    grad_key_all = matmul_tn(grad_scores, query_flat) * score_scale
    grad_query_norm = rotate(grad_query_rot, cosine, -sine_table)
    grad_query_raw, gain_query = norm_back(query_raw, head_gains[:, 0], grad_query_norm)
    grad_query = grad_query_raw.astype(bf16)
    key_grads = jnp.concatenate([grad_key_all, grad_value_all], axis=1)
    own_grads = key_grads[back * rows :]
    key_low = key_grads[: back * rows].astype(bf16)
    for by in range(1, back + 1):
        part = key_low[(back - by) * rows : (back - by + 1) * rows]
        own_grads = own_grads + shifted(part, -by).astype(f32)
    grad_key_norm = rotate(own_grads[:, :head_dim], cosine, -sine_table)
    grad_key_raw, gain_key = norm_back(key_raw, head_gains[:, 1], grad_key_norm)
    grad_key = grad_key_raw.astype(bf16)
    grad_value = own_grads[:, head_dim:].astype(bf16)
    grad_kv_a = jnp.where(c == 0, grad_key, grad_value)
    grad_kv_b = jnp.where(c == 0, grad_value, grad_key)
    grad_qkv_a = jnp.concatenate([grad_query[0], grad_query[1], grad_kv_a], axis=1)
    grad_qkv_b = jnp.concatenate([grad_query[2], grad_query[3], grad_kv_b], axis=1)
    grad_normed = matmul_nt(grad_qkv_a, attn_a[:, : 3 * head_dim]) + matmul_nt(
        grad_qkv_b, attn_b[:, : 3 * head_dim]
    )
    grad_from_norm, gain_zero = norm_back(inputs, gains[:, 0], grad_normed)
    tokens_grad = (grad_resid + grad_from_norm).astype(bf16)

    norm_part = jnp.stack(
        [jnp.sum(g, axis=0) for g in (gain_zero, gain_one, gain_two, gain_three)], axis=1
    )
    head_part = jnp.stack([jnp.sum(gain_query, axis=(0, 1)), jnp.sum(gain_key, axis=0)], axis=1)
    head_cut = head_part.reshape(NZ, NXL, NY, -1)
    head_cut = jnp.stack(
        [
            jnp.where(xl == 0, head_cut[:, 0], head_cut[:, 1]),
            jnp.where(xl == 0, head_cut[:, 1], head_cut[:, 0]),
        ],
        axis=2,
    )
    per_dp = head_cut.shape[-1]
    head_column = jnp.pad(head_cut, ((0, 0), (0, 0), (0, 0), (0, dp_rows - per_dp)))
    gain_cols = jnp.concatenate([norm_part, head_column.reshape(dim, 1)], axis=1)
    n_gain = gain_cols.shape[1]
    gain_cols = jnp.pad(gain_cols, ((0, 0), (0, 128 - n_gain))).astype(bf16)

    def weight_part(grad_qkv, att):
        return jnp.concatenate(
            [
                matmul_tn(normed, grad_qkv).astype(bf16),
                matmul_tn(grad_attn, att).astype(bf16),
                gain_cols,
            ],
            axis=1,
        )

    mine = weight_part(grad_qkv_a, attended_a).astype(f32)
    other = swap(weight_part(grad_qkv_b, attended_b), "c").astype(f32)
    part = (mine + other).astype(bf16)
    arrived = lax.all_to_all(part, ZY, 0, 0, tiled=True).reshape(NZ * NY, NXL * dp_rows, -1)
    zy_sum = jnp.sum(arrived.astype(f32), axis=0).astype(bf16)

    def columns(array, which):
        k = which * head_dim
        return jnp.concatenate(
            [
                array[:, k : k + head_dim],
                array[:, 2 * head_dim : 3 * head_dim],
                array[:, 3 * head_dim + k : 4 * head_dim + k],
                array[:, 5 * head_dim :],
            ],
            axis=1,
        )

    near, far = zy_sum[:dp_rows], zy_sum[dp_rows:]
    x_sum = (
        columns(near, 0).astype(f32)
        + swap(columns(far, 0), "xl").astype(f32)
        + swap(columns(near, 1), "xh").astype(f32)
        + swap_both(columns(far, 1)).astype(f32)
    )
    qo_share = jnp.stack(
        [x_sum[:, :head_dim], x_sum[:, 2 * head_dim : 3 * head_dim]], axis=1
    )
    kv_mine = x_sum[:, head_dim : 2 * head_dim]
    kv_other = swap(kv_mine.astype(bf16), "c").astype(f32)
    kv_mine = kv_mine.astype(bf16).astype(f32)
    kv_total = jnp.concatenate(
        [jnp.where(c == 0, kv_mine, kv_other), jnp.where(c == 0, kv_other, kv_mine)], axis=1
    )
    norm_total = x_sum[:, 3 * head_dim : 3 * head_dim + 4]
    head_total = x_sum[:per_dp, 3 * head_dim + 4].reshape(-1, 2)

    ffn_share = ffn_rows[:dp_rows].astype(f32) + swap(ffn_rows[dp_rows:], "xl").astype(f32)
    ffn_share = ffn_share.reshape(dp_rows, 3, wide)[:, :, :ff]

    def restored(array):
        return matmul_nt(array, order).astype(bf16)

    return (
        restored(mixed),
        restored(tokens_grad),
        norm_total,
        head_total,
        qo_share,
        kv_total,
        ffn_share,
    )


def solution(mesh):
    fine = Mesh(np.asarray(mesh.devices).reshape(NZ, NXL, NY, NXH, NC), ALL)
    dp, tensor = ("z", "xl", "y"), ("xh", "c")
    return jax.shard_map(
        body,
        mesh=fine,
        in_specs=(
            P(ALL, None),
            P(),
            P(),
            P(),
            P(dp, None, tensor),
            P(dp, None),
            P(dp, None, tensor),
            P(ALL, None),
        ),
        out_specs=(
            P(ALL, None),
            P(ALL, None),
            P(dp, None),
            P(dp, None),
            P(dp, None, tensor),
            P(dp, None),
            P(dp, None, tensor),
        ),
        check_vma=False,
    )
```

time: 1110 us -> 475 us (0.43)
  blocking collectives: 374 us -> 0 us
  local copies, waits for them, and re-layouts: 144 us -> 18.3 us
  waiting for transfers between devices: 395 us -> 275 us
    all_gather x2 -> x1, waiting for transfers between devices: 259 us -> 17.1 us  [body(): ffn_full = lax.all_gather(ffn_pair, ZY, axis=0, tiled=True)]
    unnamed x2 -> x0, blocking collectives: 239 us -> none
    all_to_all x2 -> x0, blocking collectives: 93.7 us -> none  [sum_at_owner(): lax.all_to_all(tiles, axis, split_axis=0, concat_axis=0, tiled=True)]
    all_to_all x7 -> x2, waiting for transfers between devices: 32.2 us -> 99.9 us  [the longest x1 52.7 us: body(): lax.all_to_all(jnp.broadcast_to(attn_pair[None], (NZ * NY, *attn_pair.sha...]
    unnamed x136 -> x178, local copies, waits for them, and re-layouts: 65.9 us -> 7.55 us
    ppermute x2 -> x27, waiting for transfers between devices: 28.2 us -> 73.6 us  [the longest x17 59.8 us: swap(): return lax.ppermute(array, axis, [(0, 1), (1, 0)])]
    psum x1 -> x0, blocking collectives: 41.3 us -> none  [body(): lax.psum(norm_share.astype(jnp.bfloat16), 'tensor').astype(jnp.float32)]
    another operation x9 -> x8, local copies, waits for them, and re-layouts: 37.8 us -> 0.93 us  [the longest x4 0.61 us: body(): jnp.stack([jnp.sum(g, axis=0) for g in (gain_zero, gain_one, gain_two, ga...]
  transfers between devices with their start and end apart: 16 -> 31, of which waited for: 8 -> 21; matrix products, arithmetic and copies ran while one was open for 26% -> 17% of each run, Pallas kernels for 0% -> 0%
where the time goes in v1:
time: 475 us; the launch traced here: 467 us
  waiting for transfers between devices  275 us (58%)
  matrix products  63.9 us (13%)
  starting transfers between devices  57.6 us (12%)
  other arithmetic  34.3 us (7%)
  local copies, waits for them, and re-layouts  18.3 us (4%)
  between operations  17.1 us (4%)
    unnamed x3, waiting for transfers between devices  84.9 us
    ppermute x17, waiting for transfers between devices, swap(): return lax.ppermute(array, axis, [(0, 1), (1, 0)])  59.8 us
    all_to_all x1, waiting for transfers between devices, body(): lax.all_to_all(jnp.broadcast_to(attn_pair[None], (NZ * NY, *attn_pair.sha...  52.7 us
    all_to_all x1, waiting for transfers between devices, body(): lax.all_to_all(part, ZY, 0, 0, tiled=True)  47.2 us
    dot_general x9, matrix products, matmul_nt(): lax.dot_general(left, right, (((1,), (1,)), ((), ())), preferred_element_...  25.8 us
    dot_general x10, matrix products, matmul(): return jnp.dot(left, right, preferred_element_type=f32)  22.7 us
    ppermute x17, starting transfers between devices, swap(): return lax.ppermute(array, axis, [(0, 1), (1, 0)])  18.8 us
    ppermute x8, starting transfers between devices, shifted(): lax.ppermute(array, ALL, [(i, i + by) for i in range(BLOCKS) if 0 <= i +...  17.7 us
  transfers between devices with their start and end apart: 31, of which 21 were waited for; matrix products, arithmetic and copies ran while one was open for 17% of the time, Pallas kernels for 0%

profile of v1, /device:TPU:1, one launch (start us, length us, event | category | flops | bytes accessed | tf_op | source)
XLA Modules:
  0.0 466.7 jit_solution(14785933936668618417)
XLA Ops:
  11.1 9.1 %collective-permute-done.10 = bf16[36,5376]{1,0:T(8,128)(2,1)S(1)} collective-permute-done((bf16[36,5376]{1,0:T(8,128)(2,1)S(1)}, bf16[36,5376]{1,0:T(8,128)(2,1)S(1)}, u32[]{:S(2)}, u32[]{:S(2)}) %collective-permute-start.10) | collective-permute-done | bytes 387104 | tf_op jit(solution)/shard_map/ppermute | solution.py:77
  31.1 7.9 %all-to-all-start = ((bf16[16,72,1280]{2,1,0:T(8,128)(2,1)}), bf16[16,72,1280]{2,1,0:T(8,128)(2,1)S(1)}, u32[]{:S(2)}, u32[]{:S(2)}) async-start(bf16[16,72,1280]{2,1,0:T(8,128)(2,1)} %broadcast_in_dim.28), calls=%async_computation | async-start | bytes 5898240 | tf_op jit(solution)/shard_map/all_to_all | solution.py:135
  39.3 52.7 %all-to-all-done = bf16[16,72,1280]{2,1,0:T(8,128)(2,1)S(1)} async-done(((bf16[16,72,1280]{2,1,0:T(8,128)(2,1)}), bf16[16,72,1280]{2,1,0:T(8,128)(2,1)S(1)}, u32[]{:S(2)}, u32[]{:S(2)}) %all-to-all-start) | async-done | bytes 2949152 | tf_op jit(solution)/shard_map/all_to_all | solution.py:135
  105.0 5.0 %collective-permute-start.6 = (bf16[128,512]{1,0:T(8,128)(2,1)S(1)}, bf16[128,512]{1,0:T(8,128)(2,1)S(1)}, u32[]{:S(2)}, u32[]{:S(2)}) collective-permute-start(bf16[128,512]{1,0:T(8,128)(2,1)S(1)} %pad_maximum_fusion.19), channel_id=1, source_target_pairs={{0,2},{1,3},{2,4},{3,5},{4,6},{5,7},{6,8},{7,9},{8,10},{9,11},{10,... | collective-permute-start | bytes 393224 | tf_op jit(solution)/shard_map/ppermute | solution.py:85
  113.9 5.7 %collective-permute-done.5 = bf16[128,512]{1,0:T(8,128)(2,1)S(1)} collective-permute-done((bf16[128,512]{1,0:T(8,128)(2,1)S(1)}, bf16[128,512]{1,0:T(8,128)(2,1)S(1)}, u32[]{:S(2)}, u32[]{:S(2)}) %collective-permute-start.5) | collective-permute-done | bytes 131104 | tf_op jit(solution)/shard_map/ppermute | solution.py:85
  127.8 7.2 %collective-permute-done.8 = bf16[128,1152]{0,1:T(8,128)(2,1)S(1)} collective-permute-done((bf16[128,1152]{0,1:T(8,128)(2,1)S(1)}, bf16[128,1152]{0,1:T(8,128)(2,1)S(1)}, u32[]{:S(2)}, u32[]{:S(2)}) %collective-permute-start.8) | collective-permute-done | bytes 294944 | tf_op jit(solution)/shard_map/ppermute | solution.py:77
  137.7 17.1 %all-gather.2.cloned.1.call-done = bf16[1152,5376]{1,0:T(8,128)(2,1)} async-done(((bf16[72,5376]{1,0:T(8,128)(2,1)}), bf16[1152,5376]{1,0:T(8,128)(2,1)}) %all-gather.2.cloned.1.call-update) | async-done | bytes 12386320 | tf_op jit(solution)/shard_map/all_gather | solution.py:139
  154.9 7.9 %fusion.3 = f32[512,3584]{1,0:T(8,128)S(1)} fusion(bf16[1152,5376]{1,0:T(8,128)(2,1)} %all-gather.2.cloned.1.call-done, bf16[256,1152]{0,1:T(8,128)(2,1)} %collective-permute-done.9, bf16[128,1152]{0,1:T(8,128)(2,1)} %copy-done.31, bf16[128,1152]{0,1:T(8,128)(2,1)} %copy-done.25), kind=kOutput, calls=%fused_computation.6 | convolution fusion | flops 4231397376 | bytes 16777216 | tf_op jit(solution)/shard_map/dot_general | solution.py:65
  169.2 9.7 %collective-permute-done.12 = bf16[128,1152]{0,1:T(8,128)(2,1)S(1)} collective-permute-done((bf16[128,1152]{0,1:T(8,128)(2,1)S(1)}, bf16[128,1152]{0,1:T(8,128)(2,1)S(1)}, u32[]{:S(2)}, u32[]{:S(2)}) %collective-permute-start.12) | collective-permute-done | bytes 294944 | tf_op jit(solution)/shard_map/ppermute | solution.py:77
  181.0 8.5 %collective-permute-done.13 = bf16[128,1152]{0,1:T(8,128)(2,1)S(1)} collective-permute-done((bf16[128,1152]{0,1:T(8,128)(2,1)S(1)}, bf16[128,1152]{0,1:T(8,128)(2,1)S(1)}, u32[]{:S(2)}, u32[]{:S(2)}) %collective-permute-start.13) | collective-permute-done | bytes 294944 | tf_op jit(solution)/shard_map/ppermute | solution.py:77
  193.6 6.4 %fusion.15 = (bf16[512,1792]{1,0:T(8,128)(2,1)S(1)}, bf16[512,1792]{1,0:T(8,128)(2,1)}) fusion(f32[512,3584]{1,0:T(8,128)S(1)} %fusion.3, bf16[1152,5376]{1,0:T(8,128)(2,1)S(1)} %copy-done.77, bf16[256,1152]{0,1:T(8,128)(2,1)S(1)} %collective-permute-done.14, bf16[128,1152]{0,1:T(8,128)(2,1)S(1)} %collective-permute-done.13, ...), kind=kOutput, calls=%fused_computation.23 | convolution fusion | flops 2139488256 | bytes 16318464 | tf_op jit(solution)/shard_map/dot_general | solution.py:65
  200.0 8.4 %fusion.29 = bf16[512,1152]{0,1:T(8,128)(2,1)S(1)} fusion(bf16[1152,5376]{1,0:T(8,128)(2,1)} %all-gather.2.cloned.1.call-done, bf16[512,1792]{1,0:T(8,128)(2,1)} %get-tuple-element.61, bf16[512,1792]{1,0:T(8,128)(2,1)S(1)} %get-tuple-element.60), kind=kOutput, calls=%fused_computation.41 | convolution fusion | flops 4235788288 | bytes 13107200 | tf_op jit(solution)/shard_map/dot_general | solution.py:69
  209.7 6.2 %convolution_convert_fusion = bf16[1152,3584]{1,0:T(8,128)(2,1)S(1)} fusion(bf16[512,1792]{1,0:T(8,128)(2,1)} %get-tuple-element.61, bf16[512,1792]{1,0:T(8,128)(2,1)S(1)} %get-tuple-element.60, bf16[256,1152]{0,1:T(8,128)(2,1)} %collective-permute-done.9, bf16[128,1152]{0,1:T(8,128)(2,1)S(1)} %copy-done.32, bf16[128,1152]{0,1:T(8,128)(2,1)S(1)} %copy-done.26), kind=kOutput, calls=%fused_computation.1 | convolution fusion | flops 4242866176 | bytes 13107200 | tf_op jit(solution)/shard_map/dot_general | solution.py:73
  222.7 5.0 %pad_maximum_fusion = bf16[1152,5376]{1,0:T(8,128)(2,1)} fusion(bf16[1152,1792]{1,0:T(8,128)(2,1)S(1)} %convolution_convert_fusion.1, bf16[1152,3584]{1,0:T(8,128)(2,1)S(1)} %convolution_convert_fusion), kind=kLoop, calls=%fused_computation.2 | loop fusion | flops 24772608 | bytes 24772608 | tf_op jit(solution)/shard_map/concatenate | solution.py:220
  227.8 4.8 %collective-permute-done.16 = bf16[128,1152]{0,1:T(8,128)(2,1)S(1)} collective-permute-done((bf16[128,1152]{0,1:T(8,128)(2,1)}, bf16[128,1152]{0,1:T(8,128)(2,1)S(1)}, u32[]{:S(2)}, u32[]{:S(2)}) %collective-permute-start.16) | collective-permute-done | bytes 294944 | tf_op jit(solution)/shard_map/ppermute | solution.py:77
  251.8 5.6 %collective-permute-done.19 = bf16[128,512]{1,0:T(8,128)(2,1)S(1)} collective-permute-done((bf16[128,512]{1,0:T(8,128)(2,1)S(1)}, bf16[128,512]{1,0:T(8,128)(2,1)S(1)}, u32[]{:S(2)}, u32[]{:S(2)}) %collective-permute-start.19) | collective-permute-done | bytes 131104 | tf_op jit(solution)/shard_map/ppermute | solution.py:85
  263.7 5.9 %fusion.25 = bf16[1152,1408]{0,1:T(8,128)(2,1)S(1)} fusion(bf16[1152,5]{0,1:T(8,128)(2,1)S(1)} %concatenate.135, bf16[1152,512]{0,1:T(8,128)(2,1)S(1)} %copy-done.5, bf16[1152,768]{0,1:T(8,128)(2,1)S(1)} %convolution_convert_fusion.2), kind=kLoop, calls=%fused_computation.37 | loop fusion | flops 12976128 | bytes 6204672 | tf_op jit(solution)/shard_map/concatenate | solution.py:290
  271.1 4.6 collective-permute-done.21
  275.7 6.1 %add_convert_fusion = bf16[1152,1408]{0,1:T(8,128)(2,1)S(1)} fusion(bf16[1152,1408]{0,1:T(8,128)(2,1)S(1)} %collective-permute-done.21, bf16[1152,5]{0,1:T(8,128)(2,1)S(1)} %copy-done.40, bf16[1152,512]{0,1:T(8,128)(2,1)S(1)} %convolution_convert_fusion.5, bf16[1152,768]{0,1:T(8,128)(2,1)S(1)} %convolution_convert_fusion.3), kind=kLoop, calls=%fused_computation.9 | loop fusion | flops 17842176 | bytes 9448704 | tf_op jit(solution)/shard_map/convert_element_type | solution.py:301
  285.4 9.3 %all-to-all-start.1 = ((bf16[16,72,1408]{2,1,0:T(8,128)(2,1)}), bf16[16,72,1408]{2,1,0:T(8,128)(2,1)S(1)}, u32[]{:S(2)}, u32[]{:S(2)}) async-start(bf16[16,72,1408]{2,1,0:T(8,128)(2,1)} %bitcast.104), calls=%async_computation.1 | async-start | bytes 6488064 | tf_op jit(solution)/shard_map/all_to_all | solution.py:302
  299.9 47.2 %all-to-all-done.1 = bf16[16,72,1408]{2,1,0:T(8,128)(2,1)S(1)} async-done(((bf16[16,72,1408]{2,1,0:T(8,128)(2,1)}), bf16[16,72,1408]{2,1,0:T(8,128)(2,1)S(1)}, u32[]{:S(2)}, u32[]{:S(2)}) %all-to-all-start.1) | async-done | bytes 3244064 | tf_op jit(solution)/shard_map/all_to_all | solution.py:302
  355.5 4.4 collective-permute-start.25
  359.9 84.8 %all-reduce.6.cloned.1.call-done = bf16[1152,5376]{1,0:T(8,128)(2,1)} async-done(((bf16[1152,5376]{1,0:T(8,128)(2,1)}), bf16[1152,5376]{1,0:T(8,128)(2,1)}) %all-reduce.6.cloned.1.call-update) | async-done | bytes 12386320
  450.1 6.7 %collective-permute-done.26 = bf16[36,5376]{1,0:T(8,128)(2,1)S(1)} collective-permute-done((bf16[36,5376]{1,0:T(8,128)(2,1)S(1)}, bf16[36,5376]{1,0:T(8,128)(2,1)S(1)}, u32[]{:S(2)}, u32[]{:S(2)}) %collective-permute-start.26) | collective-permute-done | bytes 387104 | tf_op jit(solution)/shard_map/ppermute | solution.py:77
  (368 shorter events, 113.4 us)
Async XLA Ops:
  7.2 147.7 %all-gather.2.cloned.1.call-start = ((), (), s32[]{:S(2)}) async-start(), calls=%async_computation.2 | async-start | bytes 13160448 | tf_op jit(solution)/shard_map/all_gather | solution.py:139
  9.0 11.2 %collective-permute-start.10 = (bf16[36,5376]{1,0:T(8,128)(2,1)S(1)}, bf16[36,5376]{1,0:T(8,128)(2,1)S(1)}, u32[]{:S(2)}, u32[]{:S(2)}) collective-permute-start(bf16[36,5376]{1,0:T(8,128)(2,1)S(1)} %bitcast.113), channel_id=1, source_target_pairs={{0,16},{16,0},{1,17},{17,1},{2,18},{18,2},{3,19},{19,3},{4,20},{20... | collective-permute-start | bytes 1161224 | tf_op jit(solution)/shard_map/ppermute | solution.py:77
  21.4 4.9 %collective-permute-start = (bf16[36,768]{1,0:T(8,128)(2,1)S(1)}, bf16[36,768]{1,0:T(8,128)(2,1)S(1)}, u32[]{:S(2)}, u32[]{:S(2)}) collective-permute-start(bf16[36,768]{1,0:T(8,128)(2,1)S(1)} %pad_maximum_fusion.37), channel_id=1, source_target_pairs={{0,2},{2,0},{1,3},{3,1},{4,6},{6,4},{5,7},{7,5},{8,10},{10,8},{9,1... | collective-permute-start | bytes 165896 | tf_op jit(solution)/shard_map/ppermute | solution.py:77
  31.1 60.9 %all-to-all-start = ((bf16[16,72,1280]{2,1,0:T(8,128)(2,1)}), bf16[16,72,1280]{2,1,0:T(8,128)(2,1)S(1)}, u32[]{:S(2)}, u32[]{:S(2)}) async-start(bf16[16,72,1280]{2,1,0:T(8,128)(2,1)} %broadcast_in_dim.28), calls=%async_computation | async-start | bytes 5898240 | tf_op jit(solution)/shard_map/all_to_all | solution.py:135
  39.0 405.7 %all-reduce.6.cloned.1.call-start = ((), (), s32[]{:S(2)}) async-start(), calls=%async_computation.3 | async-start | bytes 24772608
  92.0 6.7 %collective-permute-start.3 = (bf16[1152,1280]{1,0:T(8,128)(2,1)S(1)}, bf16[1152,1280]{1,0:T(8,128)(2,1)}, u32[]{:S(2)}, u32[]{:S(2)}) collective-permute-start(bf16[1152,1280]{1,0:T(8,128)(2,1)S(1)} %bitcast.105), channel_id=1, source_target_pairs={{0,1},{1,0},{2,3},{3,2},{4,5},{5,4},{6,7},{7,6},{8,9},{9,8},{10,11... | collective-permute-start | bytes 8847368 | tf_op jit(solution)/shard_map/ppermute | solution.py:77
  102.4 11.5 %collective-permute-start.4 = (bf16[128,512]{1,0:T(8,128)(2,1)S(1)}, bf16[128,512]{1,0:T(8,128)(2,1)S(1)}, u32[]{:S(2)}, u32[]{:S(2)}) collective-permute-start(bf16[128,512]{1,0:T(8,128)(2,1)S(1)} %pad_maximum_fusion.19), channel_id=1, source_target_pairs={{0,4},{1,5},{2,6},{3,7},{4,8},{5,9},{6,10},{7,11},{8,12},{9,13},{1... | collective-permute-start | bytes 393224 | tf_op jit(solution)/shard_map/ppermute | solution.py:85
  103.7 15.9 %collective-permute-start.5 = (bf16[128,512]{1,0:T(8,128)(2,1)S(1)}, bf16[128,512]{1,0:T(8,128)(2,1)S(1)}, u32[]{:S(2)}, u32[]{:S(2)}) collective-permute-start(bf16[128,512]{1,0:T(8,128)(2,1)S(1)} %pad_maximum_fusion.19), channel_id=1, source_target_pairs={{0,3},{1,4},{2,5},{3,6},{4,7},{5,8},{6,9},{7,10},{8,11},{9,12},{10... | collective-permute-start | bytes 393224 | tf_op jit(solution)/shard_map/ppermute | solution.py:85
  105.0 14.6 %collective-permute-start.6 = (bf16[128,512]{1,0:T(8,128)(2,1)S(1)}, bf16[128,512]{1,0:T(8,128)(2,1)S(1)}, u32[]{:S(2)}, u32[]{:S(2)}) collective-permute-start(bf16[128,512]{1,0:T(8,128)(2,1)S(1)} %pad_maximum_fusion.19), channel_id=1, source_target_pairs={{0,2},{1,3},{2,4},{3,5},{4,6},{5,7},{6,8},{7,9},{8,10},{9,11},{10,... | collective-permute-start | bytes 393224 | tf_op jit(solution)/shard_map/ppermute | solution.py:85
  110.0 9.7 %collective-permute-start.7 = (bf16[128,512]{1,0:T(8,128)(2,1)S(1)}, bf16[128,512]{1,0:T(8,128)(2,1)S(1)}, u32[]{:S(2)}, u32[]{:S(2)}) collective-permute-start(bf16[128,512]{1,0:T(8,128)(2,1)S(1)} %pad_maximum_fusion.19), channel_id=1, source_target_pairs={{0,1},{1,2},{2,3},{3,4},{4,5},{5,6},{6,7},{7,8},{8,9},{9,10},{10,1... | collective-permute-start | bytes 393224 | tf_op jit(solution)/shard_map/ppermute | solution.py:85
  127.6 7.3 %collective-permute-start.8 = (bf16[128,1152]{0,1:T(8,128)(2,1)S(1)}, bf16[128,1152]{0,1:T(8,128)(2,1)S(1)}, u32[]{:S(2)}, u32[]{:S(2)}) collective-permute-start(bf16[128,1152]{0,1:T(8,128)(2,1)S(1)} %multiply_convert_fusion.4), channel_id=1, source_target_pairs={{0,2},{2,0},{1,3},{3,1},{4,6},{6,4},{5,7},{7,5},{8,10},{10,8},{9,1... | collective-permute-start | bytes 884744 | tf_op jit(solution)/shard_map/ppermute | solution.py:77
  169.1 9.8 %collective-permute-start.12 = (bf16[128,1152]{0,1:T(8,128)(2,1)S(1)}, bf16[128,1152]{0,1:T(8,128)(2,1)S(1)}, u32[]{:S(2)}, u32[]{:S(2)}) collective-permute-start(bf16[128,1152]{0,1:T(8,128)(2,1)S(1)} %slice.450), channel_id=1, source_target_pairs={{0,2},{2,0},{1,3},{3,1},{4,6},{6,4},{5,7},{7,5},{8,10},{10,8},{9,1... | collective-permute-start | bytes 884744 | tf_op jit(solution)/shard_map/ppermute | solution.py:77
  180.6 8.9 %collective-permute-start.13 = (bf16[128,1152]{0,1:T(8,128)(2,1)S(1)}, bf16[128,1152]{0,1:T(8,128)(2,1)S(1)}, u32[]{:S(2)}, u32[]{:S(2)}) collective-permute-start(bf16[128,1152]{0,1:T(8,128)(2,1)S(1)} %multiply_convert_fusion.3), channel_id=1, source_target_pairs={{0,2},{2,0},{1,3},{3,1},{4,6},{6,4},{5,7},{7,5},{8,10},{10,8},{9,1... | collective-permute-start | bytes 884744 | tf_op jit(solution)/shard_map/ppermute | solution.py:77
  209.3 10.0 %collective-permute-start.15 = (bf16[256,1152]{0,1:T(8,128)(2,1)}, bf16[256,1152]{0,1:T(8,128)(2,1)}, u32[]{:S(2)}, u32[]{:S(2)}) collective-permute-start(bf16[256,1152]{0,1:T(8,128)(2,1)} %slice.453), channel_id=1, source_target_pairs={{0,1},{1,0},{2,3},{3,2},{4,5},{5,4},{6,7},{7,6},{8,9},{9,8},{10,11... | collective-permute-start | bytes 1769480 | tf_op jit(solution)/shard_map/ppermute | solution.py:77
  222.2 10.4 %collective-permute-start.16 = (bf16[128,1152]{0,1:T(8,128)(2,1)}, bf16[128,1152]{0,1:T(8,128)(2,1)S(1)}, u32[]{:S(2)}, u32[]{:S(2)}) collective-permute-start(bf16[128,1152]{0,1:T(8,128)(2,1)} %slice.455), channel_id=1, source_target_pairs={{0,2},{2,0},{1,3},{3,1},{4,6},{6,4},{5,7},{7,5},{8,10},{10,8},{9,1... | collective-permute-start | bytes 884744 | tf_op jit(solution)/shard_map/ppermute | solution.py:77
  241.8 10.0 %collective-permute-start.20 = (bf16[128,512]{1,0:T(8,128)(2,1)S(1)}, bf16[128,512]{1,0:T(8,128)(2,1)S(1)}, u32[]{:S(2)}, u32[]{:S(2)}) collective-permute-start(bf16[128,512]{1,0:T(8,128)(2,1)S(1)} %get-tuple-element.65), channel_id=1, source_target_pairs={{4,0},{5,1},{6,2},{7,3},{8,4},{9,5},{10,6},{11,7},{12,8},{13,9},{1... | collective-permute-start | bytes 393224 | tf_op jit(solution)/shard_map/ppermute | solution.py:85
  243.1 14.4 %collective-permute-start.19 = (bf16[128,512]{1,0:T(8,128)(2,1)S(1)}, bf16[128,512]{1,0:T(8,128)(2,1)S(1)}, u32[]{:S(2)}, u32[]{:S(2)}) collective-permute-start(bf16[128,512]{1,0:T(8,128)(2,1)S(1)} %get-tuple-element.66), channel_id=1, source_target_pairs={{3,0},{4,1},{5,2},{6,3},{7,4},{8,5},{9,6},{10,7},{11,8},{12,9},{13... | collective-permute-start | bytes 393224 | tf_op jit(solution)/shard_map/ppermute | solution.py:85
  244.4 13.1 %collective-permute-start.18 = (bf16[128,512]{1,0:T(8,128)(2,1)S(1)}, bf16[128,512]{1,0:T(8,128)(2,1)S(1)}, u32[]{:S(2)}, u32[]{:S(2)}) collective-permute-start(bf16[128,512]{1,0:T(8,128)(2,1)S(1)} %get-tuple-element.67), channel_id=1, source_target_pairs={{2,0},{3,1},{4,2},{5,3},{6,4},{7,5},{8,6},{9,7},{10,8},{11,9},{12,... | collective-permute-start | bytes 393224 | tf_op jit(solution)/shard_map/ppermute | solution.py:85
  245.7 11.8 %collective-permute-start.17 = (bf16[128,512]{1,0:T(8,128)(2,1)S(1)}, bf16[128,512]{1,0:T(8,128)(2,1)S(1)}, u32[]{:S(2)}, u32[]{:S(2)}) collective-permute-start(bf16[128,512]{1,0:T(8,128)(2,1)S(1)} %get-tuple-element.64), channel_id=1, source_target_pairs={{1,0},{2,1},{3,2},{4,3},{5,4},{6,5},{7,6},{8,7},{9,8},{10,9},{11,1... | collective-permute-start | bytes 393224 | tf_op jit(solution)/shard_map/ppermute | solution.py:85
  269.6 6.1 %collective-permute-start.21 = (bf16[1152,1408]{0,1:T(8,128)(2,1)S(1)}, bf16[1152,1408]{0,1:T(8,128)(2,1)S(1)}, u32[]{:S(2)}, u32[]{:S(2)}) collective-permute-start(bf16[1152,1408]{0,1:T(8,128)(2,1)S(1)} %fusion.25), channel_id=1, source_target_pairs={{0,1},{1,0},{2,3},{3,2},{4,5},{5,4},{6,7},{7,6},{8,9},{9,8},{10,11... | collective-permute-start | bytes 9732104 | tf_op jit(solution)/shard_map/ppermute | solution.py:77
  285.4 61.7 %all-to-all-start.1 = ((bf16[16,72,1408]{2,1,0:T(8,128)(2,1)}), bf16[16,72,1408]{2,1,0:T(8,128)(2,1)S(1)}, u32[]{:S(2)}, u32[]{:S(2)}) async-start(bf16[16,72,1408]{2,1,0:T(8,128)(2,1)} %bitcast.104), calls=%async_computation.1 | async-start | bytes 6488064 | tf_op jit(solution)/shard_map/all_to_all | solution.py:302
  347.7 7.3 %collective-permute-start.24 = (bf16[36,896]{1,0:T(8,128)(2,1)S(1)}, bf16[36,896]{1,0:T(8,128)(2,1)S(1)}, u32[]{:S(2)}, u32[]{:S(2)}) collective-permute-start(bf16[36,896]{1,0:T(8,128)(2,1)S(1)} %pad_maximum_fusion.35), channel_id=1, source_target_pairs={{0,18},{2,16},{16,2},{18,0},{1,19},{3,17},{17,3},{19,1},{4,22},{6,... | collective-permute-start | bytes 193544 | tf_op jit(solution)/shard_map/ppermute | solution.py:81
  355.5 93.9 %collective-permute-start.25 = (bf16[36,256]{1,0:T(8,128)(2,1)S(1)}, bf16[36,256]{1,0:T(8,128)(2,1)S(1)}, u32[]{:S(2)}, u32[]{:S(2)}) collective-permute-start(bf16[36,256]{1,0:T(8,128)(2,1)S(1)} %slice.651), channel_id=1, source_target_pairs={{0,1},{1,0},{2,3},{3,2},{4,5},{5,4},{6,7},{7,6},{8,9},{9,8},{10,11... | collective-permute-start | bytes 55304 | tf_op jit(solution)/shard_map/ppermute | solution.py:77
  445.9 10.9 %collective-permute-start.26 = (bf16[36,5376]{1,0:T(8,128)(2,1)S(1)}, bf16[36,5376]{1,0:T(8,128)(2,1)S(1)}, u32[]{:S(2)}, u32[]{:S(2)}) collective-permute-start(bf16[36,5376]{1,0:T(8,128)(2,1)S(1)} %constant_dynamic-slice_fusion), channel_id=1, source_target_pairs={{0,16},{16,0},{1,17},{17,1},{2,18},{18,2},{3,19},{19,3},{4,20},{20... | collective-permute-start | bytes 1161224 | tf_op jit(solution)/shard_map/ppermute | solution.py:77
  (87 other events, 1060.1 us)
Sparse Core Ops, SparseCore 0:
  21.4 133.4 all-gather.1
  227.9 216.8 all-reduce.5
